TPU v7x, 128 devices: a whole 4x4x4 slice. The times are simulated.
128 devices in a mesh: row: 8 (over z, y_lo), col: 16 (over y_hi, x, core).
Axes of the slice: x: 4, y: 4 (y_hi: 2, y_lo: 2; y = y_hi * 2 + y_lo), z: 4, core: 2. Of those that a mesh axis runs over, the one named last changes fastest.
Arguments:
- subspace: bfloat16 [1024, 12288], P('col', 'row')
- rotation: bfloat16 [1024, 1024], replicated, may hold values from -0.1875 to 0.1875
- block_tiles: bfloat16 [64, 31, 192, 192], P('row'), as said below
- block_cols: int32 [64, 31], P('row'), may hold values from 0 to 63, as said below
Outputs:
- filtered: bfloat16 [1024, 12288], P('col', 'row')
- gram_matrix: float32 [1024, 1024], P('col', 'row')
- rayleigh: float32 [1024, 1024], P('col', 'row')
Inputs may be any that keep to these rules, and one draw needn't show every extreme that they name: block_cols[i, 0] = i; for t < 15, block_cols[i, 2t+1] = p_t(i) and block_cols[i, 2t+2] is the inverse of p_t at i, where each p_t is a permutation of the 64 block rows. The stored matrix is symmetric: block_tiles[i, 0] is symmetric and block_tiles[i, 2t+2] is the transpose of block_tiles[j, 2t+1] for the block row j with block_cols[j, 2t+1] = i.
All inputs are finite; a program needn't handle non-finite values.
Results may differ from a plain program's by a relative error of at most 0.014.
Values may be sent and summed in bfloat16 or wider, within the bound.
A program may use at most 128 MiB of HBM per device.

v0:
```python
import jax
import jax.numpy as jnp
from jax import lax
from jax.sharding import PartitionSpec as P

DEGREE = 4


filter_center = 1.6
filter_width = 0.9


def apply_blocks(vectors, block_tiles, block_cols):
    gathered = lax.all_gather(vectors, "row", axis=1, tiled=True)
    block_width = block_tiles.shape[2]
    mode_count = vectors.shape[0]
    blocks = gathered.reshape(mode_count, gathered.shape[1] // block_width, block_width)
    picked = jnp.take(blocks, block_cols, axis=1)
    product = lax.dot_general(
        picked, block_tiles, (((2, 3), (1, 3)), ((1,), (0,))), preferred_element_type=jnp.float32
    )
    return jnp.transpose(product, (1, 0, 2)).reshape(mode_count, vectors.shape[1])


def local(subspace, rotation, block_tiles, block_cols):
    mode_count, row_count = subspace.shape
    column = lax.axis_index("col")
    own_cols = lax.dynamic_slice_in_dim(rotation, column * mode_count, mode_count, 1)
    summed = lax.dot_general(
        own_cols,
        lax.all_gather(subspace, "col", axis=0, tiled=True),
        (((0,), (0,)), ((), ())),
        preferred_element_type=jnp.float32,
    )
    rotated = summed.astype(jnp.bfloat16)
    previous = rotated
    applied = apply_blocks(previous, block_tiles, block_cols)
    current = ((applied - filter_center * previous.astype(jnp.float32)) / filter_width).astype(
        jnp.bfloat16
    )
    for level_index in range(DEGREE - 1):
        applied = apply_blocks(current, block_tiles, block_cols)
        following = 2.0 / filter_width * (
            applied - filter_center * current.astype(jnp.float32)
        ) - previous.astype(jnp.float32)
        previous = current
        current = following.astype(jnp.bfloat16)
    images = apply_blocks(current, block_tiles, block_cols).astype(jnp.bfloat16)
    gram_terms = lax.dot_general(
        current,
        lax.all_gather(current, "col", axis=0, tiled=True),
        (((1,), (1,)), ((), ())),
        preferred_element_type=jnp.float32,
    )
    image_terms = lax.dot_general(
        current,
        lax.all_gather(images, "col", axis=0, tiled=True),
        (((1,), (1,)), ((), ())),
        preferred_element_type=jnp.float32,
    )
    gram_sum, image_sum = (
        lax.psum_scatter(
            gram_terms.astype(jnp.bfloat16), "row", scatter_dimension=1, tiled=True
        ).astype(jnp.float32),
        lax.psum_scatter(
            image_terms.astype(jnp.bfloat16), "row", scatter_dimension=1, tiled=True
        ).astype(jnp.float32),
    )
    inverse_rows = 1.0 / (row_count * lax.axis_size("row"))
    return (current, gram_sum * inverse_rows, image_sum * inverse_rows)


def solution(mesh):
    return jax.shard_map(
        local,
        mesh=mesh,
        in_specs=(P("col", "row"), P(), P("row", None, None, None), P("row", None)),
        out_specs=(P("col", "row"), P("col", "row"), P("col", "row")),
        check_vma=False,
    )
```

profile of v0, /device:TPU:1, one launch (start us, length us, event | category | flops | bytes accessed | tf_op | source)
XLA Modules:
  0.0 597.9 jit_solution(15963685989785320633)
XLA Ops:
  7.2 0.7 all-gather.9.cloned.1.call-update
  8.0 58.4 %all-gather.9.cloned.1.call-done = bf16[1024,1536]{1,0:T(8,128)(2,1)} async-done(((bf16[64,1536]{1,0:T(8,128)(2,1)}), bf16[1024,1536]{1,0:T(8,128)(2,1)}) %all-gather.9.cloned.1.call-update) | async-done | bytes 3145744 | tf_op jit(solution)/shard_map/all_gather | solution.py:31
  66.4 3.3 convolution_convert_fusion
  69.8 0.7 compare_select_fusion
  70.6 0.7 compare_and_fusion
  71.3 38.4 %all-gather.11.cloned.1.call-done = bf16[64,12288]{1,0:T(8,128)(2,1)} async-done(((bf16[64,1536]{1,0:T(8,128)(2,1)}), bf16[64,12288]{1,0:T(8,128)(2,1)}) %all-gather.11.cloned.1.call-update) | async-done | bytes 1572880 | tf_op jit(solution)/shard_map/all_gather | solution.py:14
  109.7 4.6 reshape.40
  114.3 2.8 copy.26
  117.1 8.5 %gather_fusion = bf16[248,64,192]{2,1,0:T(8,128)(2,1)} fusion(bf16[64,64,192]{2,0,1:T(8,128)(2,1)S(1)} %copy.26, s32[1024]{0:T(1024)S(1)} %pad_clamp_fusion), kind=kCustom, calls=%fused_computation.clone | custom fusion | bytes 12190688 | tf_op jit(solution)/shard_map/jit(_take)/gather | solution.py:18
  125.7 14.0 %fusion.25 = f32[64,8,192]{2,0,1:T(8,128)S(1)} fusion(bf16[8,31,192,192]{3,2,1,0:T(8,128)(2,1)} %param.8, bf16[8,31,64,192]{3,2,1,0:T(8,128)(2,1)} %bitcast.78, pred[8,31]{1,0:T(8,128)(4,1)S(1)} %compare_and_fusion), kind=kOutput, calls=%fused_computation.31 | convolution fusion | flops 1173258240 | bytes 24772856 | tf_op jit(solution)/shard_map/dot_general | solution.py:19
  140.1 0.7 fusion.48
  141.3 42.7 %all-gather.13.cloned.1.call-done = bf16[64,12288]{1,0:T(8,128)(2,1)} async-done(((bf16[64,1536]{1,0:T(8,128)(2,1)}), bf16[64,12288]{1,0:T(8,128)(2,1)}) %all-gather.13.cloned.1.call-update) | async-done | bytes 1572880 | tf_op jit(solution)/shard_map/all_gather | solution.py:14
  184.0 4.6 reshape.42
  188.6 2.8 copy.28
  191.4 8.5 %gather_fusion.1 = bf16[248,64,192]{2,1,0:T(8,128)(2,1)} fusion(bf16[64,64,192]{2,0,1:T(8,128)(2,1)S(1)} %copy.28, s32[1024]{0:T(1024)S(1)} %pad_clamp_fusion), kind=kCustom, calls=%fused_computation.1.clone | custom fusion | bytes 12190688 | tf_op jit(solution)/shard_map/jit(_take)/gather | solution.py:18
  199.9 14.0 %fusion.28 = f32[64,8,192]{2,0,1:T(8,128)S(1)} fusion(bf16[8,31,192,192]{3,2,1,0:T(8,128)(2,1)} %param.8, bf16[8,31,64,192]{3,2,1,0:T(8,128)(2,1)} %bitcast.79, pred[8,31]{1,0:T(8,128)(4,1)S(1)} %compare_and_fusion), kind=kOutput, calls=%fused_computation.32 | convolution fusion | flops 1173258240 | bytes 24772856 | tf_op jit(solution)/shard_map/dot_general | solution.py:19
  214.4 0.8 fusion.49
  215.8 42.5 %all-gather.15.cloned.1.call-done = bf16[64,12288]{1,0:T(8,128)(2,1)} async-done(((bf16[64,1536]{1,0:T(8,128)(2,1)}), bf16[64,12288]{1,0:T(8,128)(2,1)}) %all-gather.15.cloned.1.call-update) | async-done | bytes 1572880 | tf_op jit(solution)/shard_map/all_gather | solution.py:14
  258.3 4.6 reshape.44
  262.9 2.8 copy.30
  265.7 8.5 %gather_fusion.2 = bf16[248,64,192]{2,1,0:T(8,128)(2,1)} fusion(bf16[64,64,192]{2,0,1:T(8,128)(2,1)S(1)} %copy.30, s32[1024]{0:T(1024)S(1)} %pad_clamp_fusion), kind=kCustom, calls=%fused_computation.2.clone | custom fusion | bytes 12190688 | tf_op jit(solution)/shard_map/jit(_take)/gather | solution.py:18
  274.2 14.0 %fusion.31 = f32[64,8,192]{2,0,1:T(8,128)S(1)} fusion(bf16[8,31,192,192]{3,2,1,0:T(8,128)(2,1)} %param.8, bf16[8,31,64,192]{3,2,1,0:T(8,128)(2,1)} %bitcast.80, pred[8,31]{1,0:T(8,128)(4,1)S(1)} %compare_and_fusion), kind=kOutput, calls=%fused_computation.33 | convolution fusion | flops 1173258240 | bytes 24772856 | tf_op jit(solution)/shard_map/dot_general | solution.py:19
  288.7 0.8 fusion.52
  289.7 42.9 %all-gather.17.cloned.1.call-done = bf16[64,12288]{1,0:T(8,128)(2,1)} async-done(((bf16[64,1536]{1,0:T(8,128)(2,1)}), bf16[64,12288]{1,0:T(8,128)(2,1)}) %all-gather.17.cloned.1.call-update) | async-done | bytes 1572880 | tf_op jit(solution)/shard_map/all_gather | solution.py:14
  332.6 4.6 reshape.46
  337.2 2.8 copy.32
  340.0 8.5 %gather_fusion.3 = bf16[248,64,192]{2,1,0:T(8,128)(2,1)} fusion(bf16[64,64,192]{2,0,1:T(8,128)(2,1)S(1)} %copy.32, s32[1024]{0:T(1024)S(1)} %pad_clamp_fusion), kind=kCustom, calls=%fused_computation.3.clone | custom fusion | bytes 12190688 | tf_op jit(solution)/shard_map/jit(_take)/gather | solution.py:18
  348.5 14.0 %fusion.34 = f32[64,8,192]{2,0,1:T(8,128)S(1)} fusion(bf16[8,31,192,192]{3,2,1,0:T(8,128)(2,1)} %param.8, bf16[8,31,64,192]{3,2,1,0:T(8,128)(2,1)} %bitcast.81, pred[8,31]{1,0:T(8,128)(4,1)S(1)} %compare_and_fusion), kind=kOutput, calls=%fused_computation.34 | convolution fusion | flops 1173258240 | bytes 24772856 | tf_op jit(solution)/shard_map/dot_general | solution.py:19
  363.0 0.8 fusion.55
  363.8 0.7 all-gather.19.cloned.1.call-update
  364.8 42.1 %all-gather.21.cloned.1.call-done = bf16[64,12288]{1,0:T(8,128)(2,1)} async-done(((bf16[64,1536]{1,0:T(8,128)(2,1)}), bf16[64,12288]{1,0:T(8,128)(2,1)}) %all-gather.21.cloned.1.call-update) | async-done | bytes 1572880 | tf_op jit(solution)/shard_map/all_gather | solution.py:14
  406.9 4.6 reshape.48
  411.5 2.8 copy.34
  414.2 8.7 %gather_fusion.4 = bf16[248,64,192]{2,1,0:T(8,128)(2,1)} fusion(bf16[64,64,192]{2,0,1:T(8,128)(2,1)S(1)} %copy.34, s32[1024]{0:T(1024)S(1)} %pad_clamp_fusion), kind=kCustom, calls=%fused_computation.4.clone | custom fusion | bytes 12190688 | tf_op jit(solution)/shard_map/jit(_take)/gather | solution.py:18
  422.9 14.2 %fusion.43 = bf16[64,8,192]{2,0,1:T(8,128)(2,1)S(1)} fusion(bf16[8,31,192,192]{3,2,1,0:T(8,128)(2,1)} %param.8, bf16[8,31,64,192]{3,2,1,0:T(8,128)(2,1)} %bitcast.77, pred[8,31]{1,0:T(8,128)(4,1)S(1)} %compare_and_fusion), kind=kOutput, calls=%fused_computation.37 | convolution fusion | flops 1173356544 | bytes 24576248 | tf_op jit(solution)/shard_map/dot_general | solution.py:19
  437.2 0.9 convert_element_type.64
  438.2 25.9 %all-gather.19.cloned.1.call-done = bf16[1024,1536]{1,0:T(8,128)(2,1)} async-done(((bf16[64,1536]{1,0:T(8,128)(2,1)}), bf16[1024,1536]{1,0:T(8,128)(2,1)}) %all-gather.19.cloned.1.call-update) | async-done | bytes 3145744 | tf_op jit(solution)/shard_map/all_gather | solution.py:51
  464.1 2.9 convolution_convert_fusion.2
  467.0 0.8 copy.41
  468.0 49.7 %all-gather.23.cloned.1.call-done = bf16[1024,1536]{1,0:T(8,128)(2,1)} async-done(((bf16[64,1536]{1,0:T(8,128)(2,1)}), bf16[1024,1536]{1,0:T(8,128)(2,1)}) %all-gather.23.cloned.1.call-update) | async-done | bytes 3145744 | tf_op jit(solution)/shard_map/all_gather | solution.py:57
  517.6 2.9 convolution_convert_fusion.1
  520.6 0.8 copy.43
  521.4 29.5 %reduce-scatter.7.cloned.1.call-done = bf16[128,64]{1,0:T(8,128)(2,1)} async-done(((bf16[1024,64]{1,0:T(8,128)(2,1)}), bf16[128,64]{1,0:T(8,128)(2,1)}) %reduce-scatter.7.cloned.1.call-update) | async-done | bytes 16400
  550.9 0.8 copy.42
  551.8 0.6 convert_multiply_fusion.4
  552.4 36.9 %reduce-scatter.9.cloned.1.call-done = bf16[128,64]{1,0:T(8,128)(2,1)} async-done(((bf16[1024,64]{1,0:T(8,128)(2,1)}), bf16[128,64]{1,0:T(8,128)(2,1)}) %reduce-scatter.9.cloned.1.call-update) | async-done | bytes 16400
  589.3 0.8 copy.44
  590.2 0.6 convert_multiply_fusion.3
  (43 shorter events, 3.9 us)
Async XLA Ops:
  7.2 59.2 %copy-start = (bf16[1024,1024]{1,0:T(8,128)(2,1)S(1)}, bf16[1024,1024]{1,0:T(8,128)(2,1)}, u32[]{:S(2)}) copy-start(bf16[1024,1024]{1,0:T(8,128)(2,1)} %param.7) | copy-start | bytes 6291460
  7.2 59.2 %all-gather.9.cloned.1.call-start = ((), (), s32[]{:S(2)}) async-start(), calls=%async_computation.2 | async-start | bytes 3342336 | tf_op jit(solution)/shard_map/all_gather | solution.py:31
  7.9 101.8 %all-gather.11.cloned.1.call-start = ((), (), s32[]{:S(2)}) async-start(), calls=%async_computation.3 | async-start | bytes 1769472 | tf_op jit(solution)/shard_map/all_gather | solution.py:14
  69.7 114.2 %all-gather.13.cloned.1.call-start = ((), (), s32[]{:S(2)}) async-start(), calls=%async_computation.4 | async-start | bytes 1769472 | tf_op jit(solution)/shard_map/all_gather | solution.py:14
  125.7 14.5 %copy-start.5 = (bf16[64,1536]{1,0:T(8,128)(2,1)S(1)}, bf16[64,1536]{1,0:T(8,128)(2,1)}, u32[]{:S(2)}) copy-start(bf16[64,1536]{1,0:T(8,128)(2,1)} %convolution_convert_fusion) | copy-start | bytes 589828
  140.9 117.4 %all-gather.15.cloned.1.call-start = ((), (), s32[]{:S(2)}) async-start(), calls=%async_computation.5 | async-start | bytes 1769472 | tf_op jit(solution)/shard_map/all_gather | solution.py:14
  199.9 14.5 %copy-start.4 = (bf16[64,1536]{1,0:T(8,128)(2,1)S(1)}, bf16[64,1536]{1,0:T(8,128)(2,1)}, u32[]{:S(2)}) copy-start(bf16[64,1536]{1,0:T(8,128)(2,1)} %fusion.48) | copy-start | bytes 589828
  215.2 117.4 %all-gather.17.cloned.1.call-start = ((), (), s32[]{:S(2)}) async-start(), calls=%async_computation.6 | async-start | bytes 1769472 | tf_op jit(solution)/shard_map/all_gather | solution.py:14
  274.2 14.5 %copy-start.3 = (bf16[64,1536]{1,0:T(8,128)(2,1)S(1)}, bf16[64,1536]{1,0:T(8,128)(2,1)}, u32[]{:S(2)}) copy-start(bf16[64,1536]{1,0:T(8,128)(2,1)} %fusion.49) | copy-start | bytes 589828
  289.5 117.4 %all-gather.21.cloned.1.call-start = ((), (), s32[]{:S(2)}) async-start(), calls=%async_computation.8 | async-start | bytes 1769472 | tf_op jit(solution)/shard_map/all_gather | solution.py:14
  348.5 14.5 %copy-start.6 = (bf16[64,1536]{1,0:T(8,128)(2,1)S(1)}, bf16[64,1536]{1,0:T(8,128)(2,1)}, u32[]{:S(2)}) copy-start(bf16[64,1536]{1,0:T(8,128)(2,1)} %fusion.52) | copy-start | bytes 589828
  363.8 100.3 %all-gather.19.cloned.1.call-start = ((), (), s32[]{:S(2)}) async-start(), calls=%async_computation.7 | async-start | bytes 3342336 | tf_op jit(solution)/shard_map/all_gather | solution.py:51
  364.5 153.1 %all-gather.23.cloned.1.call-start = ((), (), s32[]{:S(2)}) async-start(), calls=%async_computation.9 | async-start | bytes 3342336 | tf_op jit(solution)/shard_map/all_gather | solution.py:57
  422.9 41.2 %copy-start.2 = (bf16[64,1536]{1,0:T(8,128)(2,1)S(1)}, bf16[64,1536]{1,0:T(8,128)(2,1)}, u32[]{:S(2)}) copy-start(bf16[64,1536]{1,0:T(8,128)(2,1)} %fusion.55) | copy-start | bytes 589828
  422.9 167.9 %copy-start.1 = (bf16[1024,1024]{1,0:T(8,128)(2,1)S(1)}, bf16[1024,1024]{1,0:T(8,128)(2,1)}, u32[]{:S(2)}) copy-start(bf16[1024,1024]{1,0:T(8,128)(2,1)} %param.7) | copy-start | bytes 6291460
  438.2 112.8 %reduce-scatter.7.cloned.1.call-start = ((), (), s32[]{:S(2)}) async-start(), calls=%async_computation.10 | async-start | bytes 294912
  467.9 121.4 %reduce-scatter.9.cloned.1.call-start = ((), (), s32[]{:S(2)}) async-start(), calls=%async_computation.11 | async-start | bytes 294912
Sparse Core Ops, SparseCore 0:
  10.5 55.8 all-gather.8
  69.9 39.8 all-gather.10
  141.0 42.9 all-gather.12
  215.3 42.9 all-gather.14
  289.6 42.9 all-gather.16
  363.9 42.9 all-gather.20
  409.9 54.1 all-gather.18
  466.5 51.0 all-gather.22
  520.0 30.8 reduce-scatter.6
  553.2 36.0 reduce-scatter.8
where the time goes:
time: 609 us; the launch traced here: 598 us
  waiting for transfers between devices  410 us (67%)
  local copies, waits for them, and re-layouts  86.2 us (14%)
  matrix products  79.3 us (13%)
  between operations  14.6 us (2%)
    all_gather x5, waiting for transfers between devices, apply_blocks(): gathered = lax.all_gather(vectors, 'row', axis=1, tiled=True)  209 us
    dot_general x5, matrix products, apply_blocks(): lax.dot_general(picked, block_tiles, (((2, 3), (1, 3)), ((1,), (0,))), pr...  70.1 us
    unnamed x12, waiting for transfers between devices  67.9 us
    all_gather x1, waiting for transfers between devices, local(): lax.all_gather(subspace, 'col', axis=0, tiled=True)  58.4 us
    all_gather x1, waiting for transfers between devices, local(): lax.all_gather(images, 'col', axis=0, tiled=True)  49.7 us
    gather x5, local copies, waits for them, and re-layouts, apply_blocks(): picked = jnp.take(blocks, block_cols, axis=1)  42.8 us
    reshape x10, local copies, waits for them, and re-layouts, apply_blocks(): gathered.reshape(mode_count, gathered.shape[1] // block_width, block_width)  37 us
    all_gather x1, waiting for transfers between devices, local(): lax.all_gather(current, 'col', axis=0, tiled=True)  25.9 us
  transfers between devices with their start and end apart: 10, of which 10 were waited for; matrix products, arithmetic and copies ran while one was open for 7% of the time, Pallas kernels for 0%

commit v1 on v0

v1 whole, which is shorter than its diff:
```python
import functools

import jax
import jax.numpy as jnp
from jax import lax
from jax.experimental import pallas as pl
from jax.experimental.pallas import tpu as pltpu
from jax.sharding import PartitionSpec as P

MESH = pl.DeviceIdType.MESH
DEGREE = 4
CENTER = 1.6
WIDTH = 0.9
ROWS = 8
COLS = 16
BLK = 192
SLOTS = 31
PAIRS = 4
HALF = PAIRS * BLK
PIECE = HALF // COLS
LANES = 128


def swap_halves(values):
    return pltpu.roll(values, LANES // 2, 1)


def kernel(
    cols, sub, rot_hbm, tiles_hbm, filt, gram, ray,
    field0, field1, tiles, rot, packed, raw, mixed, peer, merged, every, terms, parts,
    load_sem, rot_sem, out1, in1, out2, in2, row_out, row_in,
    sib_out, sib_in, col_out, col_in, sum_out, sum_in,
):
    r = lax.axis_index("row")
    c = lax.axis_index("col")
    core = lax.rem(c, 2)
    chip = c // 2
    sibling = c + 1 - 2 * core
    f32, bf16 = jnp.float32, jnp.bfloat16
    fields = (field0, field1)
    lane = lax.broadcasted_iota(jnp.int32, (1, LANES), 1) // (LANES // 2)

    loads = [pltpu.make_async_copy(tiles_hbm.at[i], tiles.at[i], load_sem.at[i]) for i in range(8)]
    rot_load = pltpu.make_async_copy(rot_hbm, rot, rot_sem)
    rot_load.start()
    for load in loads:
        load.start()

    def send(src, dst, out_sem, in_sem, to_row, to_col):
        copy = pltpu.make_async_remote_copy(
            src_ref=src, dst_ref=dst, send_sem=out_sem, recv_sem=in_sem,
            device_id=(to_row, to_col), device_id_type=MESH,
        )
        return copy

    barrier = pltpu.get_barrier_semaphore()
    for d in range(1, COLS):
        pl.semaphore_signal(barrier, inc=1, device_id=(r, lax.rem(c + d, COLS)), device_id_type=MESH)
    for d in range(1, ROWS):
        for k in (0, 1):
            pl.semaphore_signal(
                barrier, inc=1, device_id=(lax.rem(r + d, ROWS), 2 * chip + k), device_id_type=MESH
            )

    natural = jnp.concatenate([sub[:, :HALF], sub[:, HALF:]], axis=0).astype(f32)
    packed[...] = natural.T.astype(bf16)
    for q in range(PAIRS):
        field1[PAIRS * r + q] = jnp.zeros((BLK, LANES), bf16)
    pl.semaphore_wait(barrier, COLS - 1 + 2 * (ROWS - 1))

    sends = []
    for d in range(1, COLS):
        to = lax.rem(c + d, COLS)
        copy = send(
            packed.at[pl.ds(pl.multiple_of(to * PIECE, PIECE), PIECE)], raw.at[c],
            out1.at[d], in1.at[c], r, to,
        )
        copy.start()
        sends.append(copy)
    raw[c] = packed[pl.ds(pl.multiple_of(c * PIECE, PIECE), PIECE), :]
    for d in range(1, COLS):
        src = lax.rem(c + d, COLS)
        send(packed.at[pl.ds(0, PIECE)], raw.at[src], out1.at[d], in1.at[src], r, src).wait_recv()
    rot_load.wait()
    left, right = [], []
    for e in range(COLS // 2):
        a, b = raw[2 * e].astype(f32), raw[2 * e + 1].astype(f32)
        left.append(jnp.where(lane == 0, a, swap_halves(b)))
        right.append(jnp.where(lane == 0, swap_halves(a), b))
    wide = jnp.concatenate(
        [jnp.concatenate(left, axis=1), jnp.concatenate(right, axis=1)], axis=0
    ).astype(bf16)
    rotated = jnp.dot(wide, rot[...], preferred_element_type=f32)
    for e in range(COLS // 2):
        a = rotated[:PIECE, e * LANES : (e + 1) * LANES]
        b = rotated[PIECE:, e * LANES : (e + 1) * LANES]
        mixed[2 * e] = jnp.where(lane == 0, a, swap_halves(b)).astype(bf16)
        mixed[2 * e + 1] = jnp.where(lane == 0, swap_halves(a), b).astype(bf16)

    def piece(of):
        return PAIRS * r + of // PAIRS, pl.ds(pl.multiple_of(lax.rem(of, PAIRS) * PIECE, PIECE), PIECE)

    for d in range(1, COLS):
        to = lax.rem(c + d, COLS)
        copy = send(mixed.at[to], field0.at[*piece(c)], out2.at[d], in2.at[c], r, to)
        copy.start()
        sends.append(copy)
    field0[*piece(c)] = mixed[c]
    for d in range(1, COLS):
        src = lax.rem(c + d, COLS)
        send(mixed.at[0], field0.at[*piece(src)], out2.at[d], in2.at[src], r, src).wait_recv()
    for copy in sends:
        copy.wait_send()

    def chunk_rows(q):
        return pl.ds(pl.multiple_of(q * BLK, BLK), BLK)

    def row_copy(par, q, d, src_row, to_row):
        view = fields[par].at[PAIRS * src_row + q]
        return send(view, view, row_out.at[q, d], row_in.at[par, q, src_row], to_row, c)

    def spread(par, q):
        for d in range(1, ROWS):
            row_copy(par, q, d, r, lax.rem(r + d, ROWS)).start()

    def await_all(par):
        def step(q, carry):
            for d in range(1, ROWS):
                row_copy(par, q, d, lax.rem(r + d, ROWS), r).wait_recv()
                row_copy(par, q, d, r, r).wait_send()
            return carry

        lax.fori_loop(0, PAIRS, step, 0)

    def block_row(par, i):
        total = jnp.zeros((BLK, LANES), f32)
        for s in range(SLOTS):
            col = cols[i, s]
            part = fields[par][((col >> 3) << 2) + (col & 3)]
            part = jnp.where(lane == ((col >> 2) & 1), part, jnp.zeros_like(part))
            total += jnp.dot(tiles[i, s], part, preferred_element_type=f32)
        return total + swap_halves(total)

    def applied(par, q):
        return jnp.where(lane == 0, block_row(par, q), block_row(par, q + PAIRS))

    def next_level(par, q, scale):
        now = fields[par][PAIRS * r + q].astype(f32)
        before = fields[1 - par][PAIRS * r + q].astype(f32)
        level = scale * (applied(par, q) - CENTER * now) - before
        fields[1 - par][PAIRS * r + q] = level.astype(bf16)

    lax.fori_loop(0, PAIRS, lambda q, x: (spread(0, q), x)[1], 0)
    for load in loads:
        load.wait()

    def one_level(par, scale):
        await_all(par)

        def pair(q, carry):
            next_level(par, q, scale)
            spread(1 - par, q)
            return carry

        lax.fori_loop(0, PAIRS, pair, 0)

    def two_levels(k, carry):
        one_level(0, jnp.where(k == 0, 1.0 / WIDTH, 2.0 / WIDTH))
        one_level(1, 2.0 / WIDTH)
        return carry

    lax.fori_loop(0, DEGREE // 2, two_levels, 0)

    def sib_copy(which, q):
        src = fields[which].at[PAIRS * r + q]
        return send(
            src, peer.at[which, chunk_rows(q)], sib_out.at[which, q], sib_in.at[which, q], r, sibling
        )

    def whole(which):
        return jnp.concatenate([fields[which][PAIRS * r + q] for q in range(PAIRS)], axis=0).astype(f32)

    def merge(which):
        own = whole(which)
        other = swap_halves(peer[which].astype(f32))
        return jnp.where(lane == core, own, other)

    for q in range(PAIRS):
        sib_copy(0, q).start()
    flat = whole(0).T.astype(bf16)
    filt[:, :HALF] = flat[: LANES // 2]
    filt[:, HALF:] = flat[LANES // 2 :]
    for q in range(PAIRS):
        sib_copy(0, q).wait()
    own_half = merge(0)
    every[chip] = own_half.astype(bf16)
    merged[:LANES, :] = own_half.T.astype(bf16)

    def col_copy(d, src_chip, to_chip):
        return send(
            every.at[src_chip], every.at[src_chip], col_out.at[d], col_in.at[src_chip],
            r, 2 * to_chip + core,
        )

    for d in range(1, ROWS):
        col_copy(d, chip, lax.rem(chip + d, ROWS)).start()

    await_all(0)

    def image_pair(q, carry):
        field1[PAIRS * r + q] = applied(0, q).astype(bf16)
        sib_copy(1, q).start()
        return carry

    lax.fori_loop(0, PAIRS, image_pair, 0)
    for q in range(PAIRS):
        sib_copy(1, q).wait()
    merged[LANES:, :] = merge(1).T.astype(bf16)
    for d in range(1, ROWS):
        col_copy(d, lax.rem(chip + d, ROWS), chip).wait_recv()
        col_copy(d, chip, chip).wait_send()

    for e in range(ROWS):
        product = jnp.dot(merged[...], every[e], preferred_element_type=f32).astype(bf16)
        for k in range(2):
            low = k * LANES // 2
            terms[e, k, : LANES // 2] = product[low : low + LANES // 2]
            terms[e, k, LANES // 2 :] = product[LANES + low : LANES + low + LANES // 2]

    source = 2 * r + core

    def sum_copy(n, to_row, to_core, src):
        return send(
            terms.at[to_row, to_core], parts.at[src], sum_out.at[n], sum_in.at[src],
            to_row, 2 * chip + to_core,
        )

    def member(n):
        index = lax.rem(source + n, 2 * ROWS)
        return index // 2, lax.rem(index, 2), index

    for n in range(1, 2 * ROWS):
        to_row, to_core, _ = member(n)
        sum_copy(n, to_row, to_core, source).start()
    parts[source] = terms[r, core]
    for n in range(1, 2 * ROWS):
        _, _, index = member(n)
        sum_copy(n, r, core, index).wait_recv()
        sum_copy(n, r, core, index).wait_send()
    total = parts[0].astype(f32)
    for n in range(1, 2 * ROWS):
        total += parts[n].astype(f32)
    total *= 1.0 / (ROWS * 2 * HALF)
    gram[...] = total[: LANES // 2]
    ray[...] = total[LANES // 2 :]


def local(subspace, rotation, block_tiles, block_cols):
    bf16, f32 = jnp.bfloat16, jnp.float32
    vmem = pl.BlockSpec(memory_space=pltpu.VMEM)
    dma = pltpu.SemaphoreType.DMA
    return pl.pallas_call(
        kernel,
        out_shape=(
            jax.ShapeDtypeStruct(subspace.shape, bf16),
            jax.ShapeDtypeStruct((LANES // 2, LANES), f32),
            jax.ShapeDtypeStruct((LANES // 2, LANES), f32),
        ),
        in_specs=[
            pl.BlockSpec(memory_space=pltpu.SMEM),
            vmem,
            pl.BlockSpec(memory_space=pl.ANY),
            pl.BlockSpec(memory_space=pl.ANY),
        ],
        out_specs=(vmem, vmem, vmem),
        scratch_shapes=[
            pltpu.VMEM((ROWS * PAIRS, BLK, LANES), bf16),
            pltpu.VMEM((ROWS * PAIRS, BLK, LANES), bf16),
            pltpu.VMEM(block_tiles.shape, bf16),
            pltpu.VMEM(rotation.shape, bf16),
            pltpu.VMEM((HALF, LANES), bf16),
            pltpu.VMEM((COLS, PIECE, LANES), bf16),
            pltpu.VMEM((COLS, PIECE, LANES), bf16),
            pltpu.VMEM((2, HALF, LANES), bf16),
            pltpu.VMEM((2 * LANES, HALF), bf16),
            pltpu.VMEM((ROWS, HALF, LANES), bf16),
            pltpu.VMEM((ROWS, 2, LANES, LANES), bf16),
            pltpu.VMEM((2 * ROWS, LANES, LANES), bf16),
            dma((8,)),
            dma,
            dma((COLS,)),
            dma((COLS,)),
            dma((COLS,)),
            dma((COLS,)),
            dma((PAIRS, ROWS)),
            dma((2, PAIRS, ROWS)),
            dma((2, PAIRS)),
            dma((2, PAIRS)),
            dma((ROWS,)),
            dma((ROWS,)),
            dma((2 * ROWS,)),
            dma((2 * ROWS,)),
        ],
        compiler_params=pltpu.CompilerParams(
            collective_id=0, has_side_effects=True, vmem_limit_bytes=56 * 2**20
        ),
        cost_estimate=pl.CostEstimate(flops=7_000_000_000, bytes_accessed=30_000_000, transcendentals=0),
    )(block_cols, subspace, rotation, block_tiles)


def solution(mesh):
    return jax.shard_map(
        local,
        mesh=mesh,
        in_specs=(P("col", "row"), P(), P("row", None, None, None), P("row", None)),
        out_specs=(P("col", "row"), P("col", "row"), P("col", "row")),
        check_vma=False,
    )
```

time: 609 us -> 164 us (0.27); the launches traced: 598 us -> 163 us
  waiting for transfers between devices: 410 us -> 0 us
  Pallas kernels: 0 us -> 158 us
  local copies, waits for them, and re-layouts: 86.2 us -> 4.36 us
  matrix products: 79.3 us -> 0 us
  between operations: 14.6 us -> 0.64 us
    all_gather x8 -> x0, waiting for transfers between devices: 343 us -> none  [the longest x5 209 us: apply_blocks(): gathered = lax.all_gather(vectors, 'row', axis=1, tiled=True)]
    pallas_call x0 -> x1, Pallas kernels: none -> 158 us  [local(): pl.pallas_call(kernel, out_shape=(jax.ShapeDtypeStruct(subspace.shape, bf...]
    dot_general x8 -> x0, matrix products: 79.3 us -> none  [the longest x5 70.1 us: apply_blocks(): lax.dot_general(picked, block_tiles, (((2, 3), (1, 3)), ((1,), (0,))), pr...]
    unnamed x12 -> x0, waiting for transfers between devices: 67.9 us -> none
    gather x5 -> x0, local copies, waits for them, and re-layouts: 42.8 us -> none  [apply_blocks(): picked = jnp.take(blocks, block_cols, axis=1)]
    reshape x14 -> x0, local copies, waits for them, and re-layouts: 37.7 us -> none  [the longest x10 37 us: apply_blocks(): gathered.reshape(mode_count, gathered.shape[1] // block_width, block_width)]
  transfers between devices with their start and end apart: 10 -> 0, of which waited for: 10 -> 0; matrix products, arithmetic and copies ran while one was open for 7% -> 0% of each run, Pallas kernels for 0% -> 0%
where the time goes in v1:
time: 164 us; the launch traced here: 163 us
  Pallas kernels  158 us (96%)
  local copies, waits for them, and re-layouts  4.36 us (3%)
    pallas_call x1, Pallas kernels, local(): pl.pallas_call(kernel, out_shape=(jax.ShapeDtypeStruct(subspace.shape, bf...  158 us
    unnamed x3, local copies, waits for them, and re-layouts  4.36 us

profile of v1, /device:TPU:1, one launch (start us, length us, event | category | flops | bytes accessed | tf_op | source)
XLA Modules:
  0.0 163.4 jit_solution(3691047265844170913)
XLA Ops:
  0.6 158.4 %shard_map.67 = (bf16[64,1536]{1,0:T(8,128)(2,1)}, f32[64,128]{1,0:T(8,128)}, f32[64,128]{1,0:T(8,128)}) custom-call(s32[8,31]{1,0:T(8,128)} %cols.1, bf16[64,1536]{1,0:T(8,128)(2,1)} %sub.1, bf16[1024,1024]{1,0:T(8,128)(2,1)} %rot_hbm.1, bf16[8,31,192,192]{3,2,1,0:T(8,128)(2,1)} %tiles_hbm.1), custom_call_target="tpu_custom_call" | custom-call | flops 7000000000 | bytes 30000000 | tf_op jit(solution)/shard_map/pallas_call | solution.py:262
  159.1 1.6 copy.10
  160.7 1.4 copy.11
  162.0 1.4 copy.12
